TPU v7x, 512 devices: a whole 4x8x8 slice. The times are simulated.
512 devices in a mesh: ia: 16 (over z_lo, x, core), ja: 8 (over y), ka: 4 (over z_hi).
Axes of the slice: x: 4, y: 8, z: 8 (z_hi: 4, z_lo: 2; z = z_hi * 2 + z_lo), core: 2. Of those that a mesh axis runs over, the one named last changes fastest.
Arguments:
- tensor: float32 [512, 1024, 512], P('ia', 'ja', 'ka'), may hold values from -200 to 200
- factor_b: float32 [1024, 4, 96], P(('ja', 'ka')), may hold values from -4 to 4
- factor_c: float32 [512, 4, 96], P(('ka', 'ja')), may hold values from -4 to 4
Outputs:
- factor_a: float32 [512, 4, 96], P(('ia', 'ja', 'ka'))
- weights: float32 [4, 96], replicated
All inputs are finite; a program needn't handle non-finite values.
Results may differ from a plain program's by a relative error of at most 0.0003.
Values sent between devices are 32-bit elements; how exact they have to be, the bound alone decides.
No kernel may reach another device: no remote copies, remote signals or barrier semaphores. Data moves between devices by JAX's collectives and lax.ppermute only.
A program may use at most 64 MiB of HBM per device.

v0:
```python
import jax
import jax.numpy as jnp
from jax import lax
from jax.sharding import PartitionSpec as P

highest = lax.Precision.HIGHEST


def gram_of(rows):
    return jnp.einsum(
        "jsr,jsq->srq", rows, rows, precision=highest, preferred_element_type=jnp.float32
    )


def solve_normal(rows, gram_b, gram_c):
    columns = []
    for member in range(rows.shape[1]):
        normal_mat = gram_b[member] * gram_c[member]
        factor_l = jnp.linalg.cholesky(normal_mat)
        right_side = rows[:, member, :].T
        lower_sol = lax.linalg.triangular_solve(factor_l, right_side, left_side=True, lower=True)
        upper_sol = lax.linalg.triangular_solve(
            factor_l, lower_sol, left_side=True, lower=True, transpose_a=True
        )
        columns.append(upper_sol.T)
    return jnp.stack(columns, axis=1)


def shards(tensor, factor_b, factor_c):
    rows_i, rows_j, rows_k = tensor.shape
    starts, col_count = (factor_b.shape[1], factor_b.shape[2])
    width = starts * col_count
    c_block = lax.all_gather(factor_c, "ja", axis=0, tiled=True)
    partial_value = jnp.dot(
        tensor.reshape(rows_i * rows_j, rows_k),
        c_block.reshape(rows_k, width),
        precision=highest,
        preferred_element_type=jnp.float32,
    ).reshape(rows_i, rows_j, width)
    piece = lax.all_gather(factor_b, "ka", axis=0, tiled=True)
    gram_sum = jnp.zeros((starts, col_count, col_count), jnp.float32)
    count = piece.shape[0]
    flat_rows = piece.reshape(count, width)
    mttkrp = jnp.einsum(
        "ijr,jr->ir",
        partial_value,
        flat_rows,
        precision=highest,
        preferred_element_type=jnp.float32,
    )
    mttkrp, gram_rows = (mttkrp, gram_sum)
    gram_b, gram_c = lax.psum((gram_of(factor_b), gram_of(factor_c)), ("ja", "ka"))
    slab_rows = lax.psum_scatter(mttkrp, "ja", scatter_dimension=0, tiled=True)
    owned = lax.psum_scatter(slab_rows, "ka", scatter_dimension=0, tiled=True)
    owned = owned.reshape(owned.shape[0], starts, col_count)
    factor_raw = solve_normal(owned, gram_b, gram_c)
    squares = jnp.sum(factor_raw * factor_raw, axis=0)
    total = lax.psum(squares, ("ia", "ja", "ka"))
    row_total = rows_i * lax.axis_size("ia")
    weights = jnp.sqrt(total / row_total + 1e-06)
    return (factor_raw / weights[None], weights)


def solution(mesh):
    in_specs = (P("ia", "ja", "ka"), P(("ja", "ka"), None, None), P(("ka", "ja"), None, None))
    out_specs = (P(("ia", "ja", "ka"), None, None), P())
    return jax.shard_map(shards, mesh=mesh, in_specs=in_specs, out_specs=out_specs, check_vma=False)
```

profile of v0, /device:TPU:1, one launch (start us, length us, event | category | flops | bytes accessed | tf_op | source)
XLA Modules:
  0.0 503.4 jit_solution(228719153162087754)
XLA Ops:
  7.2 0.0 all-reduce.5.cloned.1.call-start
  7.2 2.1 fusion.22
  9.3 2.1 fusion
  11.4 18.7 %all_gather.7 = f32[128,4,96]{2,1,0:T(4,128)S(1)} all-gather(f32[32,4,96]{2,1,0:T(4,128)} %param.9), channel_id=1, replica_groups=mesh['ia'=16,'ja'=8,'ka'=4] {'ka'}, dimensions={0}, use_global_device_ids=true | all-gather | bytes 245760 | tf_op jit(solution)/shard_map/all_gather | solution.py:40
  30.1 22.2 %all_gather.6 = f32[128,4,96]{2,1,0:T(4,128)S(1)} all-gather(f32[16,4,96]{2,1,0:T(4,128)} %param.10), channel_id=1, replica_groups=mesh['ia'=16,'ja'=8,'ka'=4] {'ja'}, dimensions={0}, use_global_device_ids=true | all-gather | bytes 221184 | tf_op jit(solution)/shard_map/all_gather | solution.py:33
  52.3 0.1 copy.51
  52.4 0.1 copy.52
  52.6 0.1 copy.34
  52.7 1.3 dynamic-slice
  54.0 1.3 dynamic-slice.2
  55.9 5.5 %multiply_reduce_fusion = f32[384,32]{0,1:T(8,128)S(1)} fusion(f32[384,128]{0,1:T(8,128)S(1)} %copy.52, f32[32,128,128]{2,1,0:T(8,128)S(1)} %copy-done, f32[128,384,1]{0,1,2:T(8,128)S(1)} %bitcast.141), kind=kOutput, calls=%fused_computation | convolution fusion | flops 2419052544 | bytes 2539520 | tf_op jit(solution)/shard_map/dot_general | solution.py:34
  61.4 23.5 %all-reduce = f32[32,384]{1,0:T(8,128)S(1)} all-reduce(f32[32,384]{1,0:T(8,128)S(1)} %bitcast.142), channel_id=2, replica_groups=mesh['ia'=16,'ja'=8,'ka'=4] {'ja'}, use_global_device_ids=true, to_apply=%region_4.0.clone | all-reduce | flops 12288 | bytes 98304
  84.9 9.5 %all-reduce.1 = f32[4,384]{1,0:T(4,128)S(1)} all-reduce(f32[4,384]{1,0:T(4,128)S(1)} %constant_dynamic-slice_fusion), channel_id=3, replica_groups=mesh['ia'=16,'ja'=8,'ka'=4] {'ka'}, use_global_device_ids=true, to_apply=%region_5.0.clone | all-reduce | flops 1536 | bytes 12288
  94.5 0.7 dynamic-slice_reduce_fusion
  95.1 0.1 reshape.87
  95.2 210.4 %all-reduce.5.cloned.1.call-done = (f32[4,96,96]{1,2,0:T(8,128)}, f32[4,96,96]{1,2,0:T(8,128)}) async-done(((f32[4,96,96]{1,2,0:T(8,128)}, f32[4,96,96]{1,2,0:T(8,128)}), (f32[4,96,96]{1,2,0:T(8,128)}, f32[4,96,96]{1,2,0:T(8,128)})) %all-reduce.5.cloned.1.call-update) | async-done | bytes 294928 | tf_op jit(solution)/shard_map/psum | solution.py:52
  305.6 1.0 fusion.24
  306.6 0.1 copy.33
  306.7 0.1 copy.39
  306.8 0.1 copy.38
  306.9 0.1 copy.37
  307.0 1.0 fusion.9
  308.0 8.8 %cholesky.107 = f32[96,96]{1,0:T(8,128)S(1)} custom-call(f32[96,96]{1,0:T(8,128)S(1)} %get-tuple-element.10), custom_call_target="Cholesky" | custom-call | tf_op jit(solution)/shard_map/jit(cholesky)/cholesky | solution.py:19
  316.8 0.6 compare_reduce_fusion
  317.5 0.7 fusion.5
  318.1 7.4 %custom-call.21 = f32[1,96,96]{1,2,0:T(8,128)S(1)} custom-call(f32[1,96,96]{2,1,0:T(8,128)S(1)} %fusion.5), custom_call_target="InvertDiagBlocksLowerTriangular" | custom-call | tf_op jit(solution)/shard_map/triangular_solve/custom-call.2 | solution.py:22
  325.5 0.1 convolution_bitcast_fusion
  325.6 0.2 fusion.11
  325.8 8.8 %cholesky.96 = f32[96,96]{1,0:T(8,128)S(1)} custom-call(f32[96,96]{1,0:T(8,128)S(1)} %get-tuple-element.11), custom_call_target="Cholesky" | custom-call | tf_op jit(solution)/shard_map/jit(cholesky)/cholesky | solution.py:19
  334.7 0.6 compare_reduce_fusion.1
  335.3 0.7 fusion.4
  336.0 7.4 %custom-call.19 = f32[1,96,96]{1,2,0:T(8,128)S(1)} custom-call(f32[1,96,96]{2,1,0:T(8,128)S(1)} %fusion.4), custom_call_target="InvertDiagBlocksLowerTriangular" | custom-call | tf_op jit(solution)/shard_map/triangular_solve/custom-call.2 | solution.py:22
  343.3 0.1 convolution_bitcast_fusion.1
  343.5 0.2 fusion.14
  343.7 8.8 %cholesky.85 = f32[96,96]{1,0:T(8,128)S(1)} custom-call(f32[96,96]{1,0:T(8,128)S(1)} %get-tuple-element.12), custom_call_target="Cholesky" | custom-call | tf_op jit(solution)/shard_map/jit(cholesky)/cholesky | solution.py:19
  352.5 0.6 compare_reduce_fusion.2
  353.1 0.7 fusion.3
  353.8 7.4 %custom-call.17 = f32[1,96,96]{1,2,0:T(8,128)S(1)} custom-call(f32[1,96,96]{2,1,0:T(8,128)S(1)} %fusion.3), custom_call_target="InvertDiagBlocksLowerTriangular" | custom-call | tf_op jit(solution)/shard_map/triangular_solve/custom-call.2 | solution.py:22
  361.2 0.1 convolution_bitcast_fusion.2
  361.3 0.2 fusion.17
  361.5 9.0 %cholesky.74 = f32[96,96]{1,0:T(8,128)S(1)} custom-call(f32[96,96]{1,0:T(8,128)S(1)} %get-tuple-element.9), custom_call_target="Cholesky" | custom-call | tf_op jit(solution)/shard_map/jit(cholesky)/cholesky | solution.py:19
  370.6 0.6 compare_reduce_fusion.3
  371.2 0.7 fusion.2
  371.9 7.4 %custom-call.15 = f32[1,96,96]{1,2,0:T(8,128)S(1)} custom-call(f32[1,96,96]{2,1,0:T(8,128)S(1)} %fusion.2), custom_call_target="InvertDiagBlocksLowerTriangular" | custom-call | tf_op jit(solution)/shard_map/triangular_solve/custom-call.2 | solution.py:22
  379.2 0.1 convolution_bitcast_fusion.3
  379.4 0.2 fusion.20
  379.6 116.4 %psum.23 = f32[4,96]{1,0:T(4,128)S(1)} all-reduce(f32[4,96]{1,0:T(4,128)S(1)} %fusion.36), channel_id=1, replica_groups=mesh['ia'=16,'ja'=8,'ka'=4] {'ia','ja','ka'}, use_global_device_ids=true, to_apply=%region_6.10 | all-reduce | flops 384 | bytes 3072 | tf_op jit(solution)/shard_map/psum | solution.py:58
  496.0 0.6 divide_bitcast_fusion
  (9 shorter events, 0.2 us)
Async XLA Ops:
  7.2 48.7 %copy-start = (f32[32,128,128]{2,1,0:T(8,128)S(1)}, f32[32,128,128]{2,1,0:T(8,128)}, u32[]{:S(2)}) copy-start(f32[32,128,128]{2,1,0:T(8,128)} %param.8) | copy-start | bytes 6291460
  7.2 298.5 %all-reduce.5.cloned.1.call-start = ((), (), s32[]{:S(2)}) async-start(), calls=%async_computation | async-start | bytes 786432 | tf_op jit(solution)/shard_map/psum | solution.py:52
Sparse Core Ops, SparseCore 0:
  11.5 294.0 all-reduce.4
where the time goes:
time: 504 us; the launch traced here: 503 us
  waiting for transfers between devices  210 us (42%)
  blocking collectives  190 us (38%)
  other arithmetic  72.8 us (14%)
  between operations  14.9 us (3%)
  matrix products  11 us (2%)
    psum x1, waiting for transfers between devices, shards(): lax.psum((gram_of(factor_b), gram_of(factor_c)), ('ja', 'ka'))  210 us
    psum x1, blocking collectives, shards(): total = lax.psum(squares, ('ia', 'ja', 'ka'))  116 us
    another operation x12, other arithmetic, solve_normal(): factor_l = jnp.linalg.cholesky(normal_mat)  38.1 us
    unnamed x2, blocking collectives  33 us
    another operation x8, other arithmetic, solve_normal(): lax.linalg.triangular_solve(factor_l, lower_sol, left_side=True, lower=Tr...  32 us
    all_gather x1, blocking collectives, shards(): c_block = lax.all_gather(factor_c, 'ja', axis=0, tiled=True)  22.2 us
    all_gather x1, blocking collectives, shards(): piece = lax.all_gather(factor_b, 'ka', axis=0, tiled=True)  18.7 us
  transfers between devices with their start and end apart: 1, of which 1 were waited for; matrix products, arithmetic and copies ran while one was open for 2% of the time, Pallas kernels for 0%

commit v1 on v0

--- a/solution.py
+++ b/solution.py
@@ -49,7 +49,9 @@
         preferred_element_type=jnp.float32,
     )
     mttkrp, gram_rows = (mttkrp, gram_sum)
-    gram_b, gram_c = lax.psum((gram_of(factor_b), gram_of(factor_c)), ("ja", "ka"))
+    gram_b, gram_c = lax.psum(
+        lax.psum((gram_of(factor_b), gram_of(factor_c)), "ka"), axis_name="ja"
+    )
     slab_rows = lax.psum_scatter(mttkrp, "ja", scatter_dimension=0, tiled=True)
     owned = lax.psum_scatter(slab_rows, "ka", scatter_dimension=0, tiled=True)
     owned = owned.reshape(owned.shape[0], starts, col_count)

time: 504 us -> 334 us (0.66)
  waiting for transfers between devices: 210 us -> 55.6 us
  blocking collectives: 190 us -> 176 us
    psum x1 -> x2, waiting for transfers between devices: 210 us -> 55.6 us  [the longest x1 36.6 us: shards(): lax.psum(lax.psum((gram_of(factor_b), gram_of(factor_c)), 'ka'), axis_nam...]
    psum x1, blocking collectives: 116 us -> 102 us  [shards(): total = lax.psum(squares, ('ia', 'ja', 'ka'))]
  transfers between devices with their start and end apart: 1 -> 2, of which waited for: 1 -> 2; matrix products, arithmetic and copies ran while one was open for 2% -> 3% of each run, Pallas kernels for 0% -> 0%
where the time goes in v1:
time: 334 us
  blocking collectives  176 us (53%)
  other arithmetic  72.8 us (22%)
  waiting for transfers between devices  55.6 us (17%)
  between operations  14.9 us (4%)
  matrix products  11 us (3%)
  local copies, waits for them, and re-layouts  4.02 us (1%)
    psum x1, blocking collectives, shards(): total = lax.psum(squares, ('ia', 'ja', 'ka'))  102 us
    another operation x12, other arithmetic, solve_normal(): factor_l = jnp.linalg.cholesky(normal_mat)  38.1 us
    psum x1, waiting for transfers between devices, shards(): lax.psum(lax.psum((gram_of(factor_b), gram_of(factor_c)), 'ka'), axis_nam...  36.6 us
    unnamed x2, blocking collectives  33.1 us
    another operation x8, other arithmetic, solve_normal(): lax.linalg.triangular_solve(factor_l, lower_sol, left_side=True, lower=Tr...  32 us
    all_gather x1, blocking collectives, shards(): c_block = lax.all_gather(factor_c, 'ja', axis=0, tiled=True)  21.5 us
    psum x1, waiting for transfers between devices, shards(): lax.psum((gram_of(factor_b), gram_of(factor_c)), 'ka')  18.9 us
    all_gather x1, blocking collectives, shards(): piece = lax.all_gather(factor_b, 'ka', axis=0, tiled=True)  18.7 us
  transfers between devices with their start and end apart: 2, of which 2 were waited for; matrix products, arithmetic and copies ran while one was open for 3% of the time, Pallas kernels for 0%

profile of v1, /device:TPU:1, one launch (start us, length us, event | category | flops | bytes accessed | tf_op | source)
XLA Modules:
  0.0 334.0 jit_solution(149396167900332453)
XLA Ops:
  7.2 2.1 fusion.22
  9.3 2.1 fusion
  11.5 18.7 %all_gather.7 = f32[128,4,96]{2,1,0:T(4,128)S(1)} all-gather(f32[32,4,96]{2,1,0:T(4,128)} %param.9), channel_id=1, replica_groups=mesh['ia'=16,'ja'=8,'ka'=4] {'ka'}, dimensions={0}, use_global_device_ids=true | all-gather | bytes 245760 | tf_op jit(solution)/shard_map/all_gather | solution.py:40
  30.2 0.1 copy.51
  30.3 0.1 copy.52
  30.5 21.5 %all_gather.6 = f32[128,4,96]{2,1,0:T(4,128)S(1)} all-gather(f32[16,4,96]{2,1,0:T(4,128)S(1)} %copy-done.1), channel_id=1, replica_groups=mesh['ia'=16,'ja'=8,'ka'=4] {'ja'}, dimensions={0}, use_global_device_ids=true | all-gather | bytes 221184 | tf_op jit(solution)/shard_map/all_gather | solution.py:33
  52.0 0.1 copy.34
  52.1 1.3 dynamic-slice
  53.4 1.3 dynamic-slice.2
  55.3 18.9 %all-reduce.9.cloned.1.call-done = (f32[4,96,96]{1,2,0:T(8,128)}, f32[4,96,96]{1,2,0:T(8,128)}) async-done(((f32[4,96,96]{1,2,0:T(8,128)}, f32[4,96,96]{1,2,0:T(8,128)}), (f32[4,96,96]{1,2,0:T(8,128)}, f32[4,96,96]{1,2,0:T(8,128)})) %all-reduce.9.cloned.1.call-update) | async-done | bytes 294928 | tf_op jit(solution)/shard_map/psum | solution.py:53
  74.3 5.5 %multiply_reduce_fusion = f32[384,32]{0,1:T(8,128)S(1)} fusion(f32[384,128]{0,1:T(8,128)S(1)} %copy.52, f32[32,128,128]{2,1,0:T(8,128)S(1)} %copy-done, f32[128,384,1]{0,1,2:T(8,128)S(1)} %bitcast.141), kind=kOutput, calls=%fused_computation | convolution fusion | flops 2419052544 | bytes 2539520 | tf_op jit(solution)/shard_map/dot_general | solution.py:34
  79.8 23.5 %all-reduce = f32[32,384]{1,0:T(8,128)S(1)} all-reduce(f32[32,384]{1,0:T(8,128)S(1)} %bitcast.142), channel_id=2, replica_groups=mesh['ia'=16,'ja'=8,'ka'=4] {'ja'}, use_global_device_ids=true, to_apply=%region_6.0.clone | all-reduce | flops 12288 | bytes 98304
  103.3 9.6 %all-reduce.1 = f32[4,384]{1,0:T(4,128)S(1)} all-reduce(f32[4,384]{1,0:T(4,128)S(1)} %constant_dynamic-slice_fusion), channel_id=3, replica_groups=mesh['ia'=16,'ja'=8,'ka'=4] {'ka'}, use_global_device_ids=true, to_apply=%region_7.0.clone | all-reduce | flops 1536 | bytes 12288
  112.9 0.7 dynamic-slice_reduce_fusion
  113.6 0.1 reshape.87
  113.7 36.6 %all-reduce.7.cloned.1.call-done = (f32[4,96,96]{1,2,0:T(8,128)}, f32[4,96,96]{1,2,0:T(8,128)}) async-done(((f32[4,96,96]{1,2,0:T(8,128)}, f32[4,96,96]{1,2,0:T(8,128)}), (f32[4,96,96]{1,2,0:T(8,128)}, f32[4,96,96]{1,2,0:T(8,128)})) %all-reduce.7.cloned.1.call-update) | async-done | bytes 294928 | tf_op jit(solution)/shard_map/psum | solution.py:52
  150.3 1.0 fusion.24
  151.3 0.1 copy.33
  151.4 0.1 copy.39
  151.5 0.1 copy.38
  151.6 0.1 copy.37
  151.6 1.0 fusion.9
  152.7 8.8 %cholesky.107 = f32[96,96]{1,0:T(8,128)S(1)} custom-call(f32[96,96]{1,0:T(8,128)S(1)} %get-tuple-element.12), custom_call_target="Cholesky" | custom-call | tf_op jit(solution)/shard_map/jit(cholesky)/cholesky | solution.py:19
  161.5 0.6 compare_reduce_fusion
  162.1 0.7 fusion.5
  162.8 7.4 %custom-call.21 = f32[1,96,96]{1,2,0:T(8,128)S(1)} custom-call(f32[1,96,96]{2,1,0:T(8,128)S(1)} %fusion.5), custom_call_target="InvertDiagBlocksLowerTriangular" | custom-call | tf_op jit(solution)/shard_map/triangular_solve/custom-call.2 | solution.py:22
  170.1 0.1 convolution_bitcast_fusion
  170.3 0.2 fusion.11
  170.5 8.8 %cholesky.96 = f32[96,96]{1,0:T(8,128)S(1)} custom-call(f32[96,96]{1,0:T(8,128)S(1)} %get-tuple-element.13), custom_call_target="Cholesky" | custom-call | tf_op jit(solution)/shard_map/jit(cholesky)/cholesky | solution.py:19
  179.3 0.6 compare_reduce_fusion.1
  180.0 0.7 fusion.4
  180.6 7.4 %custom-call.19 = f32[1,96,96]{1,2,0:T(8,128)S(1)} custom-call(f32[1,96,96]{2,1,0:T(8,128)S(1)} %fusion.4), custom_call_target="InvertDiagBlocksLowerTriangular" | custom-call | tf_op jit(solution)/shard_map/triangular_solve/custom-call.2 | solution.py:22
  188.0 0.1 convolution_bitcast_fusion.1
  188.1 0.2 fusion.14
  188.3 8.8 %cholesky.85 = f32[96,96]{1,0:T(8,128)S(1)} custom-call(f32[96,96]{1,0:T(8,128)S(1)} %get-tuple-element.14), custom_call_target="Cholesky" | custom-call | tf_op jit(solution)/shard_map/jit(cholesky)/cholesky | solution.py:19
  197.2 0.6 compare_reduce_fusion.2
  197.8 0.7 fusion.3
  198.5 7.4 %custom-call.17 = f32[1,96,96]{1,2,0:T(8,128)S(1)} custom-call(f32[1,96,96]{2,1,0:T(8,128)S(1)} %fusion.3), custom_call_target="InvertDiagBlocksLowerTriangular" | custom-call | tf_op jit(solution)/shard_map/triangular_solve/custom-call.2 | solution.py:22
  205.8 0.1 convolution_bitcast_fusion.2
  206.0 0.2 fusion.17
  206.2 9.0 %cholesky.74 = f32[96,96]{1,0:T(8,128)S(1)} custom-call(f32[96,96]{1,0:T(8,128)S(1)} %get-tuple-element.11), custom_call_target="Cholesky" | custom-call | tf_op jit(solution)/shard_map/jit(cholesky)/cholesky | solution.py:19
  215.2 0.6 compare_reduce_fusion.3
  215.9 0.7 fusion.2
  216.5 7.4 %custom-call.15 = f32[1,96,96]{1,2,0:T(8,128)S(1)} custom-call(f32[1,96,96]{2,1,0:T(8,128)S(1)} %fusion.2), custom_call_target="InvertDiagBlocksLowerTriangular" | custom-call | tf_op jit(solution)/shard_map/triangular_solve/custom-call.2 | solution.py:22
  223.9 0.1 convolution_bitcast_fusion.3
  224.0 0.2 fusion.20
  224.3 102.3 %psum.39 = f32[4,96]{1,0:T(4,128)S(1)} all-reduce(f32[4,96]{1,0:T(4,128)S(1)} %fusion.36), channel_id=1, replica_groups=mesh['ia'=16,'ja'=8,'ka'=4] {'ia','ja','ka'}, use_global_device_ids=true, to_apply=%region_8.12 | all-reduce | flops 384 | bytes 3072 | tf_op jit(solution)/shard_map/psum | solution.py:60
  326.6 0.6 divide_bitcast_fusion
  (14 shorter events, 0.3 us)
Async XLA Ops:
  7.2 67.1 %copy-start = (f32[32,128,128]{2,1,0:T(8,128)S(1)}, f32[32,128,128]{2,1,0:T(8,128)}, u32[]{:S(2)}) copy-start(f32[32,128,128]{2,1,0:T(8,128)} %param.8) | copy-start | bytes 6291460
  7.2 23.3 %copy-start.1 = (f32[16,4,96]{2,1,0:T(4,128)S(1)}, f32[16,4,96]{2,1,0:T(4,128)}, u32[]{:S(2)}) copy-start(f32[16,4,96]{2,1,0:T(4,128)} %param.10) | copy-start | bytes 73732
  7.2 67.1 %all-reduce.9.cloned.1.call-start = ((), (), s32[]{:S(2)}) async-start(), calls=%async_computation.1 | async-start | bytes 786432 | tf_op jit(solution)/shard_map/psum | solution.py:53
  11.4 138.9 %all-reduce.7.cloned.1.call-start = ((), (), s32[]{:S(2)}) async-start(), calls=%async_computation | async-start | bytes 786432 | tf_op jit(solution)/shard_map/psum | solution.py:52
Sparse Core Ops, SparseCore 0:
  11.5 62.6 all-reduce.8
  76.7 73.5 all-reduce.6
